TPU v7x, 32 devices: a whole 2x2x4 slice. The times are simulated.
32 devices in a mesh: grp: 2 (over y), ja: 4 (over z), ia: 4 (over x, core).
Axes of the slice: x: 2, y: 2, z: 4, core: 2. Of those that a mesh axis runs over, the one named last changes fastest.
Arguments:
- pos_vel: float32 [6, 8192], P(None, ('grp', 'ja')), parts along dimension 1, may hold values from -6 to 6
- acc_jerk: float32 [6, 8192], P(None, ('grp', 'ja')), parts along dimension 1, may hold values from -6 to 6
- mass: float32 [8192], P(('grp', 'ja')), parts along dimension 0, may hold values from 7.324219e-05 to 0.0007324219
- age: float32 [8192], P(('grp', 'ja')), parts along dimension 0, may hold values from 0.125 to 0.5
- active_local: int32 [12288], P(('grp', 'ia')), parts along dimension 0, may hold values from 0 to 1023
- active_owner: int32 [12288], P(('grp', 'ia')), parts along dimension 0, may hold values from 0 to 3
Outputs:
- state: float32 [6, 12288], P(None, ('grp', 'ia')), parts along dimension 1
- forces: float32 [7, 12288], P(None, ('grp', 'ia')), parts along dimension 1
There are 2 independent parts, one for each index of `grp`. A program takes and returns all parts, laid end to end along the dimension named above; each array names one. Nothing has to cross between parts.
All inputs are finite; a program needn't handle non-finite values.
Results may differ from a plain program's by a relative error of at most 0.0003.
Values sent between devices are 32-bit elements; how exact they have to be, the bound alone decides.
A program may use at most 64 MiB of HBM per device.

v0:
```python
import jax
import jax.numpy as jnp
from jax import lax
from jax.sharding import PartitionSpec as P

soften = 0.0004


def predict(pos_vel, acc_jerk, age):
    position = pos_vel[0:3]
    velocity = pos_vel[3:6]
    accel = acc_jerk[0:3]
    jolt = acc_jerk[3:6]
    step_len = age[None, :]
    new_pos = position + step_len * (velocity + step_len * (accel * 0.5 + step_len * jolt / 6.0))
    new_vel = velocity + step_len * (accel + step_len * jolt * 0.5)
    return jnp.concatenate([new_pos, new_vel], axis=0)


def pair_terms(targets, sources, masses):
    delta_pos = sources[0:3, :, None] - targets[0:3, None, :]
    delta_vel = sources[3:6, :, None] - targets[3:6, None, :]
    dist_sq = jnp.sum(delta_pos * delta_pos, axis=0) + soften
    inverse = lax.rsqrt(dist_sq)
    inv_sq = inverse * inverse
    weighted = masses[:, None] * inverse
    weighted_cube = weighted * inv_sq
    radial = 3.0 * jnp.sum(delta_pos * delta_vel, axis=0) * inv_sq
    accel = jnp.sum(weighted_cube[None] * delta_pos, axis=1)
    jolt = jnp.sum(weighted_cube[None] * (delta_vel - radial[None] * delta_pos), axis=1)
    potential = -jnp.sum(weighted, axis=0)
    return jnp.concatenate([accel, jolt, potential[None]], axis=0)


def block_terms(targets, sources, masses):
    count = targets.shape[1]
    width = min(512, count)
    nblocks = count // width
    src_count = sources.shape[1]
    src_width = min(512, src_count)
    src_blocks = src_count // src_width
    source_pieces = sources.reshape(6, src_blocks, src_width).transpose(1, 0, 2)
    mass_pieces = masses.reshape(src_blocks, src_width)
    pieces = targets.reshape(6, nblocks, width).transpose(1, 0, 2)

    def one_block(piece):

        def accumulate(total, parts):
            return (total + pair_terms(piece, parts[0], parts[1]), None)

        total, unused = lax.scan(
            accumulate, jnp.zeros((7, width), jnp.float32), (source_pieces, mass_pieces)
        )
        return total

    results = lax.map(one_block, pieces)
    return results.transpose(1, 0, 2).reshape(7, count)


def correct(history, forces):
    pred_pos = history[0:3]
    pred_vel = history[3:6]
    old_acc = history[6:9]
    old_jolt = history[9:12]
    step_len = history[12:13]
    new_acc = forces[0:3]
    new_jolt = forces[3:6]
    differ = old_acc - new_acc
    square = step_len * step_len
    cubed = square * step_len
    fourth = square * square
    fifth = fourth * step_len
    second = (-6.0 * differ - step_len * (4.0 * old_jolt + 2.0 * new_jolt)) / square
    third = (12.0 * differ + 6.0 * step_len * (old_jolt + new_jolt)) / cubed
    position = pred_pos + fourth / 24.0 * second + fifth / 120.0 * third
    velocity = pred_vel + cubed / 6.0 * second + fourth / 24.0 * third
    return jnp.concatenate([position, velocity], axis=0)


def local(pos_vel, acc_jerk, mass, age, active_local, active_owner):
    shard_rank = lax.axis_index("ja")
    predicted = predict(pos_vel, acc_jerk, age)
    stacked = jnp.concatenate([predicted, acc_jerk, age[None, :]], axis=0)
    picked = jnp.take(stacked, active_local, axis=1)
    owned = active_owner == shard_rank
    contrib = jnp.where(owned[None, :], picked, 0.0)
    history = lax.psum(contrib, "ja")
    partial_value = block_terms(history[0:6], predicted, mass)
    forces = lax.psum(partial_value, "ja")
    state = correct(history, forces)
    return (state, forces)


def solution(mesh):
    return jax.shard_map(
        local,
        mesh=mesh,
        in_specs=(
            P(None, ("grp", "ja")),
            P(None, ("grp", "ja")),
            P(("grp", "ja")),
            P(("grp", "ja")),
            P(("grp", "ia")),
            P(("grp", "ia")),
        ),
        out_specs=(P(None, ("grp", "ia")), P(None, ("grp", "ia"))),
        check_vma=False,
    )
```

profile of v0, /device:TPU:0, one launch (start us, length us, event | category | flops | bytes accessed | tf_op | source)
XLA Modules:
  0.0 92.5 jit_solution(16712219660879244907)
XLA Ops:
  7.2 0.0 all-reduce.2.cloned.1.call-start
  7.2 0.7 compare_select_fusion
  7.9 0.9 multiply_add_fusion.1
  8.8 0.8 pad_maximum_fusion
  9.6 0.0 copy-start.2
  9.6 0.0 copy-start.3
  9.6 0.2 copy.93
  9.8 0.0 copy-start.4
  9.9 2.6 %gather_fusion = f32[1536,13]{1,0:T(8,128)S(1)} fusion(f32[13,1024]{0,1:T(8,128)S(1)} %copy.93, s32[2048]{0:T(1024)S(1)} %pad_clamp_fusion), kind=kCustom, calls=%fused_computation | custom fusion | bytes 165888 | tf_op jit(solution)/shard_map/jit(_take)/gather | solution.py:84
  12.5 0.3 copy.94
  12.7 0.0 copy-done.2
  12.7 0.0 copy-done.3
  12.8 0.7 select_bitcast_fusion
  13.4 0.0 all-reduce.2.cloned.1.call-update
  13.4 0.0 copy-done.4
  13.5 37.1 %all-reduce.2.cloned.1.call-done = f32[13,1536]{1,0:T(8,128)} async-done(((f32[13,1536]{1,0:T(8,128)}), f32[13,1536]{1,0:T(8,128)}) %all-reduce.2.cloned.1.call-update) | async-done | bytes 79888 | tf_op jit(solution)/shard_map/psum | solution.py:87
  50.5 0.8 slice.71
  51.3 0.0 copy-start
  51.3 15.3 %while.22 = (s32[]{:T(128)}, f32[3,7,512]{2,1,0:T(8,128)S(1)}, f32[3,6,512]{2,1,0:T(8,128)S(1)}, f32[2,512]{1,0:T(2,128)S(1)}, f32[2,6,512]{2,1,0:T(8,128)S(1)},...) while((s32[]{:T(128)}, f32[3,7,512]{2,1,0:T(8,128)S(1)}, f32[3,6,512]{2,1,0:T(8,128)S(1)}, ...), condition=%wide.region_9.10_spmd, body=%wide.region_1.9_spmd.sunk | while | flops 12332038 | bytes 8612156 | solution.py:56
  51.4 5.1 %while.23 = (s32[]{:T(128)}, f32[7,512]{1,0:T(8,128)S(1)}, f32[2,512]{1,0:T(2,128)S(1)}, f32[2,6,512]{2,1,0:T(8,128)S(1)}, f32[6,512]{1,0:T(8,128)S(1)}, /*index=5*/s32[]{:T(128)}, s32[]{:T(128)}, s32[]{}) while((s32[]{:T(128)}, f32[7,512]{1,0:T(8,128)S(1)}, f32[2,512]{1,0:T(2,128)S(1)}, f32[2,6,512]{2,1,0:T(8,128)S(1)}, ...), condition=%wide.region_8.8_spmd.clone, body=%wide.region_2.7_spmd.clone.sunk | while | flops 12332036 | bytes 8554623 | solution.py:51
  51.4 1.0 %fusion.13 = (f32[512,512]{1,0:T(8,128)S(1)}, f32[512,512]{1,0:T(8,128)S(1)}) fusion(f32[3,512]{1,0:T(4,128)S(1)} %get-tuple-element.214, f32[3,512]{1,0:T(4,128)S(1)} %get-tuple-element.215, f32[3,512]{1,0:T(4,128)S(1)} %get-tuple-element.216, f32[3,512]{1,0:T(4,128)S(1)} %get-tuple-element.217), kind=kLoop, calls=%fused_computation.10.clone.1 | loop fusion | flops 4194304 | bytes 2121728 | tf_op jit(solution)/shard_map/while/body/eval_jaxpr/while/body/eval_jaxpr/reduce_sum | solution.py:28
  52.4 0.3 multiply_multiply_fusion.5
  52.7 1.1 %fusion.14 = (f32[3,512]{1,0:T(4,128)S(1)}, f32[3,512]{1,0:T(4,128)S(1)}) fusion(f32[512,512]{1,0:T(8,128)S(1)} %get-tuple-element.221, f32[3,512]{1,0:T(4,128)S(1)} %get-tuple-element.216, f32[3,512]{1,0:T(4,128)S(1)} %get-tuple-element.217, f32[512,512]{1,0:T(8,128)S(1)} %get-tuple-element.222, f32[3,512]{1,0:T(4,128)S(1)} %get-tuple-element.214, ...), kind=kLoop, calls=%fused_computation.9.clone.1 | loop fusion | flops 6288384 | bytes 2134016 | tf_op jit(solution)/shard_map/while/body/eval_jaxpr/while/body/eval_jaxpr/reduce_sum | solution.py:29
  54.0 1.0 %fusion.13 = (f32[512,512]{1,0:T(8,128)S(1)}, f32[512,512]{1,0:T(8,128)S(1)}) fusion(f32[3,512]{1,0:T(4,128)S(1)} %get-tuple-element.214, f32[3,512]{1,0:T(4,128)S(1)} %get-tuple-element.215, f32[3,512]{1,0:T(4,128)S(1)} %get-tuple-element.216, f32[3,512]{1,0:T(4,128)S(1)} %get-tuple-element.217), kind=kLoop, calls=%fused_computation.10.clone.1 | loop fusion | flops 4194304 | bytes 2121728 | tf_op jit(solution)/shard_map/while/body/eval_jaxpr/while/body/eval_jaxpr/reduce_sum | solution.py:28
  54.9 0.3 multiply_multiply_fusion.5
  55.3 1.1 %fusion.14 = (f32[3,512]{1,0:T(4,128)S(1)}, f32[3,512]{1,0:T(4,128)S(1)}) fusion(f32[512,512]{1,0:T(8,128)S(1)} %get-tuple-element.221, f32[3,512]{1,0:T(4,128)S(1)} %get-tuple-element.216, f32[3,512]{1,0:T(4,128)S(1)} %get-tuple-element.217, f32[512,512]{1,0:T(8,128)S(1)} %get-tuple-element.222, f32[3,512]{1,0:T(4,128)S(1)} %get-tuple-element.214, ...), kind=kLoop, calls=%fused_computation.9.clone.1 | loop fusion | flops 6288384 | bytes 2134016 | tf_op jit(solution)/shard_map/while/body/eval_jaxpr/while/body/eval_jaxpr/reduce_sum | solution.py:29
  56.5 5.1 %while.23 = (s32[]{:T(128)}, f32[7,512]{1,0:T(8,128)S(1)}, f32[2,512]{1,0:T(2,128)S(1)}, f32[2,6,512]{2,1,0:T(8,128)S(1)}, f32[6,512]{1,0:T(8,128)S(1)}, /*index=5*/s32[]{:T(128)}, s32[]{:T(128)}, s32[]{}) while((s32[]{:T(128)}, f32[7,512]{1,0:T(8,128)S(1)}, f32[2,512]{1,0:T(2,128)S(1)}, f32[2,6,512]{2,1,0:T(8,128)S(1)}, ...), condition=%wide.region_8.8_spmd.clone, body=%wide.region_2.7_spmd.clone.sunk | while | flops 12332036 | bytes 8554623 | solution.py:51
  56.5 1.0 %fusion.13 = (f32[512,512]{1,0:T(8,128)S(1)}, f32[512,512]{1,0:T(8,128)S(1)}) fusion(f32[3,512]{1,0:T(4,128)S(1)} %get-tuple-element.214, f32[3,512]{1,0:T(4,128)S(1)} %get-tuple-element.215, f32[3,512]{1,0:T(4,128)S(1)} %get-tuple-element.216, f32[3,512]{1,0:T(4,128)S(1)} %get-tuple-element.217), kind=kLoop, calls=%fused_computation.10.clone.1 | loop fusion | flops 4194304 | bytes 2121728 | tf_op jit(solution)/shard_map/while/body/eval_jaxpr/while/body/eval_jaxpr/reduce_sum | solution.py:28
  57.5 0.3 multiply_multiply_fusion.5
  57.8 1.1 %fusion.14 = (f32[3,512]{1,0:T(4,128)S(1)}, f32[3,512]{1,0:T(4,128)S(1)}) fusion(f32[512,512]{1,0:T(8,128)S(1)} %get-tuple-element.221, f32[3,512]{1,0:T(4,128)S(1)} %get-tuple-element.216, f32[3,512]{1,0:T(4,128)S(1)} %get-tuple-element.217, f32[512,512]{1,0:T(8,128)S(1)} %get-tuple-element.222, f32[3,512]{1,0:T(4,128)S(1)} %get-tuple-element.214, ...), kind=kLoop, calls=%fused_computation.9.clone.1 | loop fusion | flops 6288384 | bytes 2134016 | tf_op jit(solution)/shard_map/while/body/eval_jaxpr/while/body/eval_jaxpr/reduce_sum | solution.py:29
  59.1 1.0 %fusion.13 = (f32[512,512]{1,0:T(8,128)S(1)}, f32[512,512]{1,0:T(8,128)S(1)}) fusion(f32[3,512]{1,0:T(4,128)S(1)} %get-tuple-element.214, f32[3,512]{1,0:T(4,128)S(1)} %get-tuple-element.215, f32[3,512]{1,0:T(4,128)S(1)} %get-tuple-element.216, f32[3,512]{1,0:T(4,128)S(1)} %get-tuple-element.217), kind=kLoop, calls=%fused_computation.10.clone.1 | loop fusion | flops 4194304 | bytes 2121728 | tf_op jit(solution)/shard_map/while/body/eval_jaxpr/while/body/eval_jaxpr/reduce_sum | solution.py:28
  60.1 0.3 multiply_multiply_fusion.5
  60.4 1.1 %fusion.14 = (f32[3,512]{1,0:T(4,128)S(1)}, f32[3,512]{1,0:T(4,128)S(1)}) fusion(f32[512,512]{1,0:T(8,128)S(1)} %get-tuple-element.221, f32[3,512]{1,0:T(4,128)S(1)} %get-tuple-element.216, f32[3,512]{1,0:T(4,128)S(1)} %get-tuple-element.217, f32[512,512]{1,0:T(8,128)S(1)} %get-tuple-element.222, f32[3,512]{1,0:T(4,128)S(1)} %get-tuple-element.214, ...), kind=kLoop, calls=%fused_computation.9.clone.1 | loop fusion | flops 6288384 | bytes 2134016 | tf_op jit(solution)/shard_map/while/body/eval_jaxpr/while/body/eval_jaxpr/reduce_sum | solution.py:29
  61.6 5.1 %while.23 = (s32[]{:T(128)}, f32[7,512]{1,0:T(8,128)S(1)}, f32[2,512]{1,0:T(2,128)S(1)}, f32[2,6,512]{2,1,0:T(8,128)S(1)}, f32[6,512]{1,0:T(8,128)S(1)}, /*index=5*/s32[]{:T(128)}, s32[]{:T(128)}, s32[]{}) while((s32[]{:T(128)}, f32[7,512]{1,0:T(8,128)S(1)}, f32[2,512]{1,0:T(2,128)S(1)}, f32[2,6,512]{2,1,0:T(8,128)S(1)}, ...), condition=%wide.region_8.8_spmd.clone, body=%wide.region_2.7_spmd.clone.sunk | while | flops 12332036 | bytes 8554623 | solution.py:51
  61.7 1.0 %fusion.13 = (f32[512,512]{1,0:T(8,128)S(1)}, f32[512,512]{1,0:T(8,128)S(1)}) fusion(f32[3,512]{1,0:T(4,128)S(1)} %get-tuple-element.214, f32[3,512]{1,0:T(4,128)S(1)} %get-tuple-element.215, f32[3,512]{1,0:T(4,128)S(1)} %get-tuple-element.216, f32[3,512]{1,0:T(4,128)S(1)} %get-tuple-element.217), kind=kLoop, calls=%fused_computation.10.clone.1 | loop fusion | flops 4194304 | bytes 2121728 | tf_op jit(solution)/shard_map/while/body/eval_jaxpr/while/body/eval_jaxpr/reduce_sum | solution.py:28
  62.6 0.3 multiply_multiply_fusion.5
  63.0 1.1 %fusion.14 = (f32[3,512]{1,0:T(4,128)S(1)}, f32[3,512]{1,0:T(4,128)S(1)}) fusion(f32[512,512]{1,0:T(8,128)S(1)} %get-tuple-element.221, f32[3,512]{1,0:T(4,128)S(1)} %get-tuple-element.216, f32[3,512]{1,0:T(4,128)S(1)} %get-tuple-element.217, f32[512,512]{1,0:T(8,128)S(1)} %get-tuple-element.222, f32[3,512]{1,0:T(4,128)S(1)} %get-tuple-element.214, ...), kind=kLoop, calls=%fused_computation.9.clone.1 | loop fusion | flops 6288384 | bytes 2134016 | tf_op jit(solution)/shard_map/while/body/eval_jaxpr/while/body/eval_jaxpr/reduce_sum | solution.py:29
  64.2 1.0 %fusion.13 = (f32[512,512]{1,0:T(8,128)S(1)}, f32[512,512]{1,0:T(8,128)S(1)}) fusion(f32[3,512]{1,0:T(4,128)S(1)} %get-tuple-element.214, f32[3,512]{1,0:T(4,128)S(1)} %get-tuple-element.215, f32[3,512]{1,0:T(4,128)S(1)} %get-tuple-element.216, f32[3,512]{1,0:T(4,128)S(1)} %get-tuple-element.217), kind=kLoop, calls=%fused_computation.10.clone.1 | loop fusion | flops 4194304 | bytes 2121728 | tf_op jit(solution)/shard_map/while/body/eval_jaxpr/while/body/eval_jaxpr/reduce_sum | solution.py:28
  65.2 0.3 multiply_multiply_fusion.5
  65.5 1.1 %fusion.14 = (f32[3,512]{1,0:T(4,128)S(1)}, f32[3,512]{1,0:T(4,128)S(1)}) fusion(f32[512,512]{1,0:T(8,128)S(1)} %get-tuple-element.221, f32[3,512]{1,0:T(4,128)S(1)} %get-tuple-element.216, f32[3,512]{1,0:T(4,128)S(1)} %get-tuple-element.217, f32[512,512]{1,0:T(8,128)S(1)} %get-tuple-element.222, f32[3,512]{1,0:T(4,128)S(1)} %get-tuple-element.214, ...), kind=kLoop, calls=%fused_computation.9.clone.1 | loop fusion | flops 6288384 | bytes 2134016 | tf_op jit(solution)/shard_map/while/body/eval_jaxpr/while/body/eval_jaxpr/reduce_sum | solution.py:29
  66.7 18.1 %psum.15 = f32[7,1536]{1,0:T(8,128)S(1)} all-reduce(f32[7,1536]{1,0:T(8,128)S(1)} %bitcast.36), channel_id=1, replica_groups=mesh['grp'=2,'ja'=4,'ia'=4] {'ja'}, use_global_device_ids=true, to_apply=%region_10.11 | all-reduce | flops 10752 | bytes 86016 | tf_op jit(solution)/shard_map/psum | solution.py:89
  84.8 0.0 copy-done
  84.8 0.0 copy-start.1
  84.8 0.1 multiply_reduce_fusion.3
  85.0 0.1 fusion.6
  85.1 0.6 pad_maximum_fusion.1
  85.7 0.0 copy-done.1
  (45 shorter events, 0.4 us)
Async XLA Ops:
  7.2 43.4 %all-reduce.2.cloned.1.call-start = ((), (), s32[]{:S(2)}) async-start(), calls=%async_computation | async-start | bytes 196608 | tf_op jit(solution)/shard_map/psum | solution.py:87
  9.6 3.1 %copy-start.2 = (s32[1536]{0:T(1024)S(1)}, s32[1536]{0:T(1024)}, u32[]{:S(2)}) copy-start(s32[1536]{0:T(1024)} %param.14) | copy-start | bytes 18436
  9.6 3.1 %copy-start.3 = (s32[1536]{0:T(1024)S(1)}, s32[1536]{0:T(1024)}, u32[]{:S(2)}) copy-start(s32[1536]{0:T(1024)} %param.15) | copy-start | bytes 18436
  9.8 3.6 %copy-start.4 = (f32[1024]{0:T(1024)S(1)}, f32[1024]{0:T(1024)}, u32[]{:S(2)}) copy-start(f32[1024]{0:T(1024)} %param.12) | copy-start | bytes 12292
  51.3 33.5 %copy-start = (f32[13,1536]{1,0:T(8,128)S(1)}, f32[13,1536]{1,0:T(8,128)}, u32[]{:S(2)}) copy-start(f32[13,1536]{1,0:T(8,128)} %all-reduce.2.cloned.1.call-done) | copy-start | bytes 239620
  84.8 0.9 copy-start.1
Sparse Core Ops, SparseCore 0:
  13.5 36.9 all-reduce.1
where the time goes:
time: 92.9 us; the launch traced here: 92.5 us
  waiting for transfers between devices  37.1 us (40%)
  other arithmetic  18.4 us (20%)
  blocking collectives  18.1 us (19%)
  between operations  14.2 us (15%)
  local copies, waits for them, and re-layouts  4.12 us (4%)
    psum x1, waiting for transfers between devices, local(): history = lax.psum(contrib, 'ja')  37.1 us
    psum x1, blocking collectives, local(): forces = lax.psum(partial_value, 'ja')  18.1 us
    reduce_sum x6, other arithmetic, pair_terms(): accel = jnp.sum(weighted_cube[None] * delta_pos, axis=1)  6.74 us
    reduce_sum x6, other arithmetic, pair_terms(): radial = 3.0 * jnp.sum(delta_pos * delta_vel, axis=0) * inv_sq  5.85 us
    gather x2, local copies, waits for them, and re-layouts, local(): picked = jnp.take(stacked, active_local, axis=1)  2.86 us
    mul x6, other arithmetic, pair_terms(): weighted_cube = weighted * inv_sq  1.86 us
  transfers between devices with their start and end apart: 1, of which 1 were waited for; matrix products, arithmetic and copies ran while one was open for 0% of the time, Pallas kernels for 0%

commit v1 on v0

--- a/solution.py
+++ b/solution.py
@@ -1,9 +1,192 @@
+import functools
 import jax
 import jax.numpy as jnp
 from jax import lax
+from jax.experimental import pallas as pl
+from jax.experimental.pallas import tpu as pltpu
 from jax.sharding import PartitionSpec as P
 
 soften = 0.0004
+LANES = 128
+SUB = 8
+MESH = pl.DeviceIdType.MESH
+
+
+def pick_columns(blocks, where_block, lane, per_block):
+    total = None
+    for b, tile in enumerate(blocks):
+        got = jnp.take_along_axis(tile, lane, axis=1, mode="promise_in_bounds")
+        total = got if total is None else jnp.where(where_block == b, got, total)
+    return total
+
+
+def force_kernel(
+    n, chunks, unroll,
+    pv, aj, mass, age, slot, owner, state_out, forces_out,
+    src_all, old_all, cols, targets, results,
+    src_send, src_recv, old_send, old_recv, res_send, res_recv,
+):
+    me = lax.axis_index("ja")
+    stars = pv.shape[1]
+    tiles = stars // LANES
+    width = chunks * LANES
+
+    barrier = pltpu.get_barrier_semaphore()
+    for s in range(1, n):
+        pl.semaphore_signal(
+            barrier, inc=1, device_id={"ja": lax.rem(me + s, n)}, device_id_type=MESH
+        )
+
+    h = age[...]
+    x, v = pv[0:3, :], pv[3:6, :]
+    a, j = aj[0:3, :], aj[3:6, :]
+    mine = src_all.at[me]
+    mine[0:3, :] = x + h * (v + h * (a * 0.5 + h * j / 6.0))
+    mine[3:6, :] = v + h * (a + h * j * 0.5)
+    mine[6:7, :] = mass[...]
+    mine[7:8, :] = h
+    old_all.at[me][...] = aj[...]
+
+    pl.semaphore_wait(barrier, n - 1)
+
+    def exchange(ref, send, recv, s, block):
+        return pltpu.make_async_remote_copy(
+            src_ref=ref.at[block], dst_ref=ref.at[block],
+            send_sem=send.at[s - 1], recv_sem=recv.at[s - 1],
+            device_id={"ja": lax.rem(me + s, n)}, device_id_type=MESH,
+        )
+
+    order = list(range(n - 1, 0, -1))
+    for s in order:
+        exchange(src_all, src_send, src_recv, s, me).start()
+    for s in order:
+        exchange(old_all, old_send, old_recv, s, me).start()
+    for s in order:
+        exchange(src_all, src_send, src_recv, s, lax.rem(me + n - s, n)).wait_recv()
+
+    def table(ref, rows):
+        return [
+            ref[b // tiles, 0:rows, (b % tiles) * LANES:(b % tiles + 1) * LANES]
+            for b in range(n * tiles)
+        ]
+
+    for b, tile in enumerate(table(src_all, SUB)):
+        cols[b * LANES:(b + 1) * LANES, :] = tile.T
+
+    def places(c):
+        start = pl.multiple_of(me * width + c * LANES, LANES)
+        local = slot[:, pl.ds(start, LANES)]
+        block = owner[:, pl.ds(start, LANES)] * tiles + local // LANES
+        lane = local % LANES
+        return (
+            jnp.broadcast_to(block, (SUB, LANES)),
+            jnp.broadcast_to(lane, (SUB, LANES)),
+        )
+
+    picked = []
+    for c in range(chunks):
+        block, lane = places(c)
+        got = pick_columns(table(src_all, SUB), block, lane, tiles)
+        picked.append(got)
+        for row in range(6):
+            targets[c, row] = jnp.broadcast_to(got[row:row + 1, :], (SUB, LANES))
+
+    def group(g, totals):
+        totals = list(totals)
+        for k in range(unroll):
+            start = pl.multiple_of((g * unroll + k) * SUB, SUB)
+            piece = cols[pl.ds(start, SUB), :]
+            qx, qy, qz, wx, wy, wz, m = [
+                jnp.broadcast_to(piece[:, i:i + 1], (SUB, LANES)) for i in range(7)
+            ]
+            for c in range(chunks):
+                rx, ry, rz = qx - targets[c, 0], qy - targets[c, 1], qz - targets[c, 2]
+                ex, ey, ez = wx - targets[c, 3], wy - targets[c, 4], wz - targets[c, 5]
+                d = (rx * rx + ry * ry) + (rz * rz + soften)
+                z = lax.rsqrt(d)
+                zz = z * z
+                weight = m * z
+                cube = weight * zz
+                radial = ((rx * ex + ry * ey) + rz * ez) * zz
+                fifth = cube * radial
+                t = totals[7 * c:7 * c + 7]
+                totals[7 * c:7 * c + 7] = [
+                    t[0] + cube * rx, t[1] + cube * ry, t[2] + cube * rz,
+                    t[3] + (cube * ex - 3.0 * (fifth * rx)),
+                    t[4] + (cube * ey - 3.0 * (fifth * ry)),
+                    t[5] + (cube * ez - 3.0 * (fifth * rz)),
+                    t[6] + weight,
+                ]
+        return tuple(totals)
+
+    zero = jnp.zeros((SUB, LANES), jnp.float32)
+    totals = lax.fori_loop(0, n * stars // (SUB * unroll), group, (zero,) * (7 * chunks))
+
+    for s in order:
+        exchange(old_all, old_send, old_recv, s, lax.rem(me + n - s, n)).wait_recv()
+
+    for c in range(chunks):
+        sums = [jnp.sum(t, axis=0, keepdims=True) for t in totals[7 * c:7 * c + 7]]
+        new_acc = jnp.concatenate(sums[0:3], axis=0)
+        new_jolt = jnp.concatenate(sums[3:6], axis=0)
+        block, lane = places(c)
+        old = pick_columns(table(old_all, SUB), block, lane, tiles)
+        got = picked[c]
+        step = got[7:8, :]
+        old_acc, old_jolt = old[0:3, :], old[3:6, :]
+        differ = old_acc - new_acc
+        second = -6.0 * differ - step * (4.0 * old_jolt + 2.0 * new_jolt)
+        third = 12.0 * differ + 6.0 * step * (old_jolt + new_jolt)
+        place = results.at[me]
+        lanes = slice(c * LANES, (c + 1) * LANES)
+        place[0:3, lanes] = new_acc
+        place[3:6, lanes] = new_jolt
+        place[6:7, lanes] = -sums[6]
+        place[7:8, lanes] = step
+        place[8:11, lanes] = got[0:3, :] + step * step * (second / 24.0 + third / 120.0)
+        place[11:14, lanes] = got[3:6, :] + step * (second / 6.0 + third / 24.0)
+        place[14:16, lanes] = jnp.zeros((2, LANES), jnp.float32)
+
+    for s in order:
+        exchange(results, res_send, res_recv, s, me).start()
+    for s in order:
+        exchange(results, res_send, res_recv, s, lax.rem(me + n - s, n)).wait_recv()
+    for k in range(n):
+        forces_out[:, k * width:(k + 1) * width] = results[k, 0:7, :]
+        state_out[:, k * width:(k + 1) * width] = results[k, 8:14, :]
+    for s in order:
+        exchange(src_all, src_send, src_recv, s, me).wait_send()
+        exchange(old_all, old_send, old_recv, s, me).wait_send()
+        exchange(results, res_send, res_recv, s, me).wait_send()
+
+
+def fused(n, pos_vel, acc_jerk, mass, age, active_local, active_owner):
+    stars = pos_vel.shape[1]
+    count = active_local.shape[0]
+    chunks = count // (n * LANES)
+    pairs = n * stars * chunks * LANES
+    vmem = pl.BlockSpec(memory_space=pltpu.VMEM)
+    old = jnp.concatenate([acc_jerk, acc_jerk[0:2]], axis=0)
+    return pl.pallas_call(
+        functools.partial(force_kernel, n, chunks, 2),
+        out_shape=(
+            jax.ShapeDtypeStruct((6, count), jnp.float32),
+            jax.ShapeDtypeStruct((7, count), jnp.float32),
+        ),
+        in_specs=[vmem] * 6,
+        out_specs=(vmem, vmem),
+        scratch_shapes=[
+            pltpu.VMEM((n, SUB, stars), jnp.float32),
+            pltpu.VMEM((n, SUB, stars), jnp.float32),
+            pltpu.VMEM((n * stars, SUB), jnp.float32),
+            pltpu.VMEM((chunks, 6, SUB, LANES), jnp.float32),
+            pltpu.VMEM((n, 16, chunks * LANES), jnp.float32),
+        ] + [pltpu.SemaphoreType.DMA((n - 1,))] * 6,
+        compiler_params=pltpu.CompilerParams(
+            collective_id=0, has_side_effects=True, vmem_limit_bytes=32 * 1024 * 1024
+        ),
+        cost_estimate=pl.CostEstimate(flops=41 * pairs, bytes_accessed=0, transcendentals=pairs),
+    )(pos_vel, old, mass[None, :], age[None, :], active_local[None, :], active_owner[None, :])
 
 
 def predict(pos_vel, acc_jerk, age):
@@ -92,8 +275,16 @@
 
 
 def solution(mesh):
+    n = mesh.shape["ja"]
+
+    def run(*args):
+        count, stars = args[4].shape[0], args[0].shape[1]
+        if n > 1 and count % (n * LANES) == 0 and stars % LANES == 0:
+            return fused(n, *args)
+        return local(*args)
+
     return jax.shard_map(
-        local,
+        run,
         mesh=mesh,
         in_specs=(
             P(None, ("grp", "ja")),

time: 92.9 us -> 50.2 us (0.54)
  Pallas kernels: 0 us -> 45.1 us
  waiting for transfers between devices: 37.1 us -> 0 us
  other arithmetic: 18.4 us -> 0.01 us
  blocking collectives: 18.1 us -> 0 us
  between operations: 14.2 us -> 0.66 us
    pallas_call x0 -> x1, Pallas kernels: none -> 45.1 us  [fused(): pl.pallas_call(functools.partial(force_kernel, n, chunks, 2), out_shape=(...]
    psum x1 -> x0, waiting for transfers between devices: 37.1 us -> none  [local(): history = lax.psum(contrib, 'ja')]
    psum x1 -> x0, blocking collectives: 18.1 us -> none  [local(): forces = lax.psum(partial_value, 'ja')]
    reduce_sum x12 -> x0, other arithmetic: 12.6 us -> none  [the longest x6 6.74 us: pair_terms(): accel = jnp.sum(weighted_cube[None] * delta_pos, axis=1)]
    gather x2 -> x0, local copies, waits for them, and re-layouts: 2.86 us -> none  [local(): picked = jnp.take(stacked, active_local, axis=1)]
    unnamed x10, local copies, waits for them, and re-layouts: 0.03 us -> 2 us
    mul x6 -> x0, other arithmetic: 1.86 us -> none  [pair_terms(): weighted_cube = weighted * inv_sq]
    concatenate x3 -> x1, other arithmetic: 1.45 us -> 0.01 us  [fused(): old = jnp.concatenate([acc_jerk, acc_jerk[0:2]], axis=0)]
  transfers between devices with their start and end apart: 1 -> 0, of which waited for: 1 -> 0; matrix products, arithmetic and copies ran while one was open for 0% -> 0% of each run, Pallas kernels for 0% -> 0%
where the time goes in v1:
time: 50.2 us; the launch traced here: 49.9 us
  Pallas kernels  45.1 us (90%)
  local copies, waits for them, and re-layouts  4.1 us (8%)
  between operations  0.66 us (1%)
    pallas_call x1, Pallas kernels, fused(): pl.pallas_call(functools.partial(force_kernel, n, chunks, 2), out_shape=(...  45.1 us
    unnamed x10, local copies, waits for them, and re-layouts  2 us

profile of v1, /device:TPU:0, one launch (start us, length us, event | category | flops | bytes accessed | tf_op | source)
XLA Modules:
  0.0 49.9 jit_solution(10448482588052750365)
XLA Ops:
  0.6 0.0 copy-start.3
  0.6 0.7 %broadcast_in_dim.14.slot = s32[1,1536]{1,0:T(1,128)S(1)} reshape(s32[1536]{0:T(1024)} %param.10) | data formatting | bytes 12288 | tf_op jit(solution)/shard_map/broadcast_in_dim | solution.py:189
  1.3 0.7 %broadcast_in_dim.15.owner = s32[1,1536]{1,0:T(1,128)S(1)} reshape(s32[1536]{0:T(1024)} %param.11) | data formatting | bytes 12288 | tf_op jit(solution)/shard_map/broadcast_in_dim | solution.py:189
  2.1 0.0 slice-start
  2.1 0.0 copy-done.3
  2.1 0.7 %slice-done = f32[2,1024]{1,0:T(2,128)S(1)} async-done(((f32[6,1024]{1,0:T(8,128)}), f32[2,1024]{1,0:T(2,128)S(1)}, s32[]{:S(2)}) %slice-start) | async-done | bytes 8216 | tf_op jit(solution)/shard_map/slice | solution.py:169
  2.7 0.0 copy-start
  2.8 0.0 copy-start.1
  2.8 0.0 copy-start.2
  2.8 0.7 %copy-done = f32[6,1024]{1,0:T(8,128)S(1)} copy-done((f32[6,1024]{1,0:T(8,128)S(1)}, f32[6,1024]{1,0:T(8,128)}, u32[]{:S(2)}) %copy-start) | copy-done | bytes 24600
  3.5 0.0 copy-done.1
  3.5 0.0 copy-done.2
  3.5 45.1 %shard_map.77 = (f32[6,1536]{1,0:T(8,128)S(1)}, f32[7,1536]{1,0:T(8,128)S(1)}) custom-call(f32[6,1024]{1,0:T(8,128)S(1)} %copy-done, f32[8,1024]{1,0:T(8,128)S(1)} %pad_maximum_fusion.aj, f32[1,1024]{1,0:T(1,128)S(1)} %bitcast.2, f32[1,1024]{1,0:T(1,128)S(1)} %bitcast.3, s32[1,1536]{1,0:T(1,128)S(1)} %broadcast_in_dim.14.slot, ...), custom_call_target="tpu_custom_call" | custom-call | flops 64487424 | tf_op jit(solution)/shard_map/pallas_call | solution.py:170
  48.6 0.6 %copy.10 = f32[6,1536]{1,0:T(8,128)} copy(f32[6,1536]{1,0:T(8,128)S(1)} %get-tuple-element.4) | data formatting | bytes 73728
  49.3 0.6 %copy.11 = f32[7,1536]{1,0:T(8,128)} copy(f32[7,1536]{1,0:T(8,128)S(1)} %get-tuple-element.5) | data formatting | bytes 86016
  (1 shorter events, 0.0 us)
Async XLA Ops:
  0.6 1.4 %copy-start.3 = (f32[6,1024]{1,0:T(8,128)S(1)}, f32[6,1024]{1,0:T(8,128)}, u32[]{:S(2)}) copy-start(f32[6,1024]{1,0:T(8,128)} %param.7) | copy-start | bytes 73732
  2.1 0.7 %slice-start = ((f32[6,1024]{1,0:T(8,128)}), f32[2,1024]{1,0:T(2,128)S(1)}, s32[]{:S(2)}) async-start(f32[6,1024]{1,0:T(8,128)} %param.7), calls=%async_computation | async-start | bytes 16384 | tf_op jit(solution)/shard_map/slice | solution.py:169
  2.7 0.8 %copy-start = (f32[6,1024]{1,0:T(8,128)S(1)}, f32[6,1024]{1,0:T(8,128)}, u32[]{:S(2)}) copy-start(f32[6,1024]{1,0:T(8,128)} %pv.1) | copy-start | bytes 73732
  2.8 0.8 %copy-start.1 = (f32[1024]{0:T(1024)S(1)}, f32[1024]{0:T(1024)}, u32[]{:S(2)}) copy-start(f32[1024]{0:T(1024)} %param.8) | copy-start | bytes 12292
  2.8 0.8 %copy-start.2 = (f32[1024]{0:T(1024)S(1)}, f32[1024]{0:T(1024)}, u32[]{:S(2)}) copy-start(f32[1024]{0:T(1024)} %param.9) | copy-start | bytes 12292

commit v2 on v1

--- a/solution.py
+++ b/solution.py
@@ -12,7 +12,7 @@
 MESH = pl.DeviceIdType.MESH
 
 
-def pick_columns(blocks, where_block, lane, per_block):
+def pick_columns(blocks, where_block, lane):
     total = None
     for b, tile in enumerate(blocks):
         got = jnp.take_along_axis(tile, lane, axis=1, mode="promise_in_bounds")
@@ -21,15 +21,15 @@
 
 
 def force_kernel(
-    n, chunks, unroll,
+    n, chunks, pair_rows,
     pv, aj, mass, age, slot, owner, state_out, forces_out,
-    src_all, old_all, cols, targets, results,
+    src_all, old_all, wide, picked, targets, sums, results,
     src_send, src_recv, old_send, old_recv, res_send, res_recv,
 ):
     me = lax.axis_index("ja")
     stars = pv.shape[1]
     tiles = stars // LANES
-    width = chunks * LANES
+    rows = pair_rows * SUB
 
     barrier = pltpu.get_barrier_semaphore()
     for s in range(1, n):
@@ -45,7 +45,9 @@
     mine[3:6, :] = v + h * (a + h * j * 0.5)
     mine[6:7, :] = mass[...]
     mine[7:8, :] = h
-    old_all.at[me][...] = aj[...]
+    old = old_all.at[me]
+    old[0:6, :] = aj[...]
+    old[6:8, :] = jnp.zeros((2, stars), jnp.float32)
 
     pl.semaphore_wait(barrier, n - 1)
 
@@ -56,117 +58,158 @@
             device_id={"ja": lax.rem(me + s, n)}, device_id_type=MESH,
         )
 
+    def exchange_result(s, block, c):
+        at = c * (n - 1) + (s - 1)
+        return pltpu.make_async_remote_copy(
+            src_ref=results.at[block, c], dst_ref=results.at[block, c],
+            send_sem=res_send.at[at], recv_sem=res_recv.at[at],
+            device_id={"ja": lax.rem(me + s, n)}, device_id_type=MESH,
+        )
+
+    def widen(block):
+        for b in range(tiles):
+            tile = src_all[block, :, b * LANES:(b + 1) * LANES]
+            for i in range(7):
+                wide[block * tiles + b, i] = jnp.broadcast_to(tile[i:i + 1, :], (SUB, LANES))
+
     order = list(range(n - 1, 0, -1))
     for s in order:
         exchange(src_all, src_send, src_recv, s, me).start()
     for s in order:
         exchange(old_all, old_send, old_recv, s, me).start()
-    for s in order:
-        exchange(src_all, src_send, src_recv, s, lax.rem(me + n - s, n)).wait_recv()
-
-    def table(ref, rows):
+    widen(me)
+    for s in range(1, n):
+        block = lax.rem(me + n - s, n)
+        exchange(src_all, src_send, src_recv, s, block).wait_recv()
+        widen(block)
+
+    def table(ref):
         return [
-            ref[b // tiles, 0:rows, (b % tiles) * LANES:(b % tiles + 1) * LANES]
+            ref[b // tiles, :, (b % tiles) * LANES:(b % tiles + 1) * LANES]
             for b in range(n * tiles)
         ]
 
-    for b, tile in enumerate(table(src_all, SUB)):
-        cols[b * LANES:(b + 1) * LANES, :] = tile.T
-
     def places(c):
-        start = pl.multiple_of(me * width + c * LANES, LANES)
-        local = slot[:, pl.ds(start, LANES)]
-        block = owner[:, pl.ds(start, LANES)] * tiles + local // LANES
+        at = pl.ds(me * chunks + c, 1)
+        local = slot[at, :]
+        block = owner[at, :] * tiles + local // LANES
         lane = local % LANES
         return (
             jnp.broadcast_to(block, (SUB, LANES)),
             jnp.broadcast_to(lane, (SUB, LANES)),
         )
 
-    picked = []
     for c in range(chunks):
         block, lane = places(c)
-        got = pick_columns(table(src_all, SUB), block, lane, tiles)
-        picked.append(got)
-        for row in range(6):
-            targets[c, row] = jnp.broadcast_to(got[row:row + 1, :], (SUB, LANES))
-
-    def group(g, totals):
-        totals = list(totals)
-        for k in range(unroll):
-            start = pl.multiple_of((g * unroll + k) * SUB, SUB)
-            piece = cols[pl.ds(start, SUB), :]
-            qx, qy, qz, wx, wy, wz, m = [
-                jnp.broadcast_to(piece[:, i:i + 1], (SUB, LANES)) for i in range(7)
-            ]
-            for c in range(chunks):
-                rx, ry, rz = qx - targets[c, 0], qy - targets[c, 1], qz - targets[c, 2]
-                ex, ey, ez = wx - targets[c, 3], wy - targets[c, 4], wz - targets[c, 5]
-                d = (rx * rx + ry * ry) + (rz * rz + soften)
-                z = lax.rsqrt(d)
-                zz = z * z
-                weight = m * z
-                cube = weight * zz
-                radial = ((rx * ex + ry * ey) + rz * ez) * zz
-                fifth = cube * radial
-                t = totals[7 * c:7 * c + 7]
-                totals[7 * c:7 * c + 7] = [
-                    t[0] + cube * rx, t[1] + cube * ry, t[2] + cube * rz,
-                    t[3] + (cube * ex - 3.0 * (fifth * rx)),
-                    t[4] + (cube * ey - 3.0 * (fifth * ry)),
-                    t[5] + (cube * ez - 3.0 * (fifth * rz)),
-                    t[6] + weight,
-                ]
-        return tuple(totals)
-
-    zero = jnp.zeros((SUB, LANES), jnp.float32)
-    totals = lax.fori_loop(0, n * stars // (SUB * unroll), group, (zero,) * (7 * chunks))
-
-    for s in order:
-        exchange(old_all, old_send, old_recv, s, lax.rem(me + n - s, n)).wait_recv()
-
-    for c in range(chunks):
-        sums = [jnp.sum(t, axis=0, keepdims=True) for t in totals[7 * c:7 * c + 7]]
-        new_acc = jnp.concatenate(sums[0:3], axis=0)
-        new_jolt = jnp.concatenate(sums[3:6], axis=0)
+        got = pick_columns(table(src_all), block, lane)
+        picked[c] = got
+        turned = got.T
+        for t in range(LANES // SUB):
+            for i in range(6):
+                targets[c * (LANES // SUB) + t, i] = jnp.broadcast_to(
+                    turned[t * SUB:(t + 1) * SUB, i:i + 1], (SUB, LANES)
+                )
+
+    def chunk(c, carry):
+        def few(t, carry):
+            first = (c * (LANES // rows) + t) * pair_rows
+            aims = [[targets[first + k, i] for i in range(6)] for k in range(pair_rows)]
+
+            def tile(b, totals):
+                qx, qy, qz, wx, wy, wz, m = [wide[b, i] for i in range(7)]
+                news = []
+                for k in range(pair_rows):
+                    px, py, pz, ux, uy, uz = aims[k]
+                    rx, ry, rz = qx - px, qy - py, qz - pz
+                    ex, ey, ez = wx - ux, wy - uy, wz - uz
+                    d = (rx * rx + ry * ry) + (rz * rz + soften)
+                    z = lax.rsqrt(d)
+                    zz = z * z
+                    weight = m * z
+                    cube = weight * zz
+                    radial = ((rx * ex + ry * ey) + rz * ez) * zz
+                    ax, ay, az = cube * rx, cube * ry, cube * rz
+                    terms = (
+                        ax, ay, az, cube * ex, cube * ey, cube * ez,
+                        radial * ax, radial * ay, radial * az, weight,
+                    )
+                    news += [p + q for p, q in zip(totals[10 * k:10 * k + 10], terms)]
+                return tuple(news)
+
+            zero = jnp.zeros((SUB, LANES), jnp.float32)
+            count = n * tiles
+            totals = lax.fori_loop(0, count, tile, (zero,) * (10 * pair_rows), unroll=count)
+            for k in range(pair_rows):
+                at = pl.ds(pl.multiple_of(t * rows + k * SUB, SUB), SUB)
+                v = totals[10 * k:10 * k + 10]
+                for i in range(3):
+                    sums[i, at, :] = v[i]
+                    sums[3 + i, at, :] = v[3 + i] - 3.0 * v[6 + i]
+                sums[6, at, :] = v[9]
+            return carry
+
+        lax.fori_loop(0, LANES // rows, few, 0)
+
+        @pl.when(c == 0)
+        def _():
+            for s in order:
+                exchange(old_all, old_send, old_recv, s, lax.rem(me + n - s, n)).wait_recv()
+
+        ones = jnp.ones((SUB, LANES), jnp.float32)
+        total = [
+            lax.dot_general(
+                ones, sums[q], (((1,), (1,)), ((), ())),
+                precision=lax.Precision.HIGHEST, preferred_element_type=jnp.float32,
+            )[0:1, :]
+            for q in range(7)
+        ]
+        new_acc = jnp.concatenate(total[0:3], axis=0)
+        new_jolt = jnp.concatenate(total[3:6], axis=0)
         block, lane = places(c)
-        old = pick_columns(table(old_all, SUB), block, lane, tiles)
+        old = pick_columns(table(old_all), block, lane)
         got = picked[c]
         step = got[7:8, :]
         old_acc, old_jolt = old[0:3, :], old[3:6, :]
         differ = old_acc - new_acc
         second = -6.0 * differ - step * (4.0 * old_jolt + 2.0 * new_jolt)
         third = 12.0 * differ + 6.0 * step * (old_jolt + new_jolt)
-        place = results.at[me]
-        lanes = slice(c * LANES, (c + 1) * LANES)
-        place[0:3, lanes] = new_acc
-        place[3:6, lanes] = new_jolt
-        place[6:7, lanes] = -sums[6]
-        place[7:8, lanes] = step
-        place[8:11, lanes] = got[0:3, :] + step * step * (second / 24.0 + third / 120.0)
-        place[11:14, lanes] = got[3:6, :] + step * (second / 6.0 + third / 24.0)
-        place[14:16, lanes] = jnp.zeros((2, LANES), jnp.float32)
-
-    for s in order:
-        exchange(results, res_send, res_recv, s, me).start()
-    for s in order:
-        exchange(results, res_send, res_recv, s, lax.rem(me + n - s, n)).wait_recv()
+        place = results.at[me, c]
+        place[0:3, :] = new_acc
+        place[3:6, :] = new_jolt
+        place[6:7, :] = -total[6]
+        place[7:8, :] = step
+        place[8:11, :] = got[0:3, :] + step * step * (second / 24.0 + third / 120.0)
+        place[11:14, :] = got[3:6, :] + step * (second / 6.0 + third / 24.0)
+        place[14:16, :] = jnp.zeros((2, LANES), jnp.float32)
+        for s in order:
+            exchange_result(s, me, c).start()
+        return carry
+
+    lax.fori_loop(0, chunks, chunk, 0)
+
+    for c in range(chunks):
+        for s in order:
+            exchange_result(s, lax.rem(me + n - s, n), c).wait_recv()
     for k in range(n):
-        forces_out[:, k * width:(k + 1) * width] = results[k, 0:7, :]
-        state_out[:, k * width:(k + 1) * width] = results[k, 8:14, :]
+        for c in range(chunks):
+            at = (k * chunks + c) * LANES
+            forces_out[:, at:at + LANES] = results[k, c, 0:7, :]
+            state_out[:, at:at + LANES] = results[k, c, 8:14, :]
     for s in order:
         exchange(src_all, src_send, src_recv, s, me).wait_send()
         exchange(old_all, old_send, old_recv, s, me).wait_send()
-        exchange(results, res_send, res_recv, s, me).wait_send()
+        for c in range(chunks):
+            exchange_result(s, me, c).wait_send()
 
 
 def fused(n, pos_vel, acc_jerk, mass, age, active_local, active_owner):
     stars = pos_vel.shape[1]
     count = active_local.shape[0]
     chunks = count // (n * LANES)
+    groups = chunks * LANES // SUB
     pairs = n * stars * chunks * LANES
     vmem = pl.BlockSpec(memory_space=pltpu.VMEM)
-    old = jnp.concatenate([acc_jerk, acc_jerk[0:2]], axis=0)
+    dma = pltpu.SemaphoreType.DMA
     return pl.pallas_call(
         functools.partial(force_kernel, n, chunks, 2),
         out_shape=(
@@ -178,15 +221,20 @@
         scratch_shapes=[
             pltpu.VMEM((n, SUB, stars), jnp.float32),
             pltpu.VMEM((n, SUB, stars), jnp.float32),
-            pltpu.VMEM((n * stars, SUB), jnp.float32),
-            pltpu.VMEM((chunks, 6, SUB, LANES), jnp.float32),
-            pltpu.VMEM((n, 16, chunks * LANES), jnp.float32),
-        ] + [pltpu.SemaphoreType.DMA((n - 1,))] * 6,
+            pltpu.VMEM((n * stars // LANES, 7, SUB, LANES), jnp.float32),
+            pltpu.VMEM((chunks, SUB, LANES), jnp.float32),
+            pltpu.VMEM((groups, 6, SUB, LANES), jnp.float32),
+            pltpu.VMEM((7, LANES, LANES), jnp.float32),
+            pltpu.VMEM((n, chunks, 16, LANES), jnp.float32),
+        ] + [dma((n - 1,))] * 4 + [dma(((n - 1) * chunks,))] * 2,
         compiler_params=pltpu.CompilerParams(
             collective_id=0, has_side_effects=True, vmem_limit_bytes=32 * 1024 * 1024
         ),
         cost_estimate=pl.CostEstimate(flops=41 * pairs, bytes_accessed=0, transcendentals=pairs),
-    )(pos_vel, old, mass[None, :], age[None, :], active_local[None, :], active_owner[None, :])
+    )(
+        pos_vel, acc_jerk, mass[None, :], age[None, :],
+        active_local.reshape(-1, LANES), active_owner.reshape(-1, LANES),
+    )
 
 
 def predict(pos_vel, acc_jerk, age):

time: 50.2 us -> 34 us (0.68)
  Pallas kernels: 45.1 us -> 27.4 us
  local copies, waits for them, and re-layouts: 4.1 us -> 5.52 us
    pallas_call x1, Pallas kernels: 45.1 us -> 27.4 us  [fused(): pl.pallas_call(functools.partial(force_kernel, n, chunks, 2), out_shape=(...]
    unnamed x10 -> x14, local copies, waits for them, and re-layouts: 2 us -> 5.52 us
    broadcast_in_dim x2 -> x0, local copies, waits for them, and re-layouts: 1.41 us -> none  [the longest x1 0.71 us: fused(): active_local[None, :]]
    slice x2 -> x0, local copies, waits for them, and re-layouts: 0.69 us -> none  [fused(): old = jnp.concatenate([acc_jerk, acc_jerk[0:2]], axis=0)]
where the time goes in v2:
time: 34 us; the launch traced here: 33.6 us
  Pallas kernels  27.4 us (81%)
  local copies, waits for them, and re-layouts  5.52 us (16%)
  between operations  0.65 us (2%)
    pallas_call x1, Pallas kernels, fused(): pl.pallas_call(functools.partial(force_kernel, n, chunks, 2), out_shape=(...  27.4 us
    unnamed x14, local copies, waits for them, and re-layouts  5.52 us

profile of v2, /device:TPU:0, one launch (start us, length us, event | category | flops | bytes accessed | tf_op | source)
XLA Modules:
  0.0 33.6 jit_solution(12431610448459366218)
XLA Ops:
  0.6 0.0 copy-start.4
  0.6 0.7 %copy-done.4 = f32[1024]{0:T(1024)S(1)} copy-done((f32[1024]{0:T(1024)S(1)}, f32[1024]{0:T(1024)}, u32[]{:S(2)}) %copy-start.4) | copy-done | bytes 4120
  1.3 0.0 copy-start
  1.3 0.8 %copy-done = f32[6,1024]{1,0:T(8,128)S(1)} copy-done((f32[6,1024]{1,0:T(8,128)S(1)}, f32[6,1024]{1,0:T(8,128)}, u32[]{:S(2)}) %copy-start) | copy-done | bytes 24600
  2.1 0.0 copy-start.1
  2.1 0.8 %copy-done.1 = f32[6,1024]{1,0:T(8,128)S(1)} copy-done((f32[6,1024]{1,0:T(8,128)S(1)}, f32[6,1024]{1,0:T(8,128)}, u32[]{:S(2)}) %copy-start.1) | copy-done | bytes 24600
  2.8 0.0 copy-start.2
  2.8 0.7 %copy-done.2 = s32[1536]{0:T(1024)S(1)} copy-done((s32[1536]{0:T(1024)S(1)}, s32[1536]{0:T(1024)}, u32[]{:S(2)}) %copy-start.2) | copy-done | bytes 6168
  3.5 0.0 copy-start.3
  3.5 0.7 %copy-done.3 = s32[1536]{0:T(1024)S(1)} copy-done((s32[1536]{0:T(1024)S(1)}, s32[1536]{0:T(1024)}, u32[]{:S(2)}) %copy-start.3) | copy-done | bytes 6168
  4.2 0.0 copy-start.5
  4.2 0.7 %copy-done.5 = f32[1024]{0:T(1024)S(1)} copy-done((f32[1024]{0:T(1024)S(1)}, f32[1024]{0:T(1024)}, u32[]{:S(2)}) %copy-start.5) | copy-done | bytes 4120
  4.9 27.4 %shard_map.77 = (f32[6,1536]{1,0:T(8,128)S(1)}, f32[7,1536]{1,0:T(8,128)S(1)}) custom-call(f32[6,1024]{1,0:T(8,128)S(1)} %copy-done, f32[6,1024]{1,0:T(8,128)S(1)} %copy-done.1, f32[1,1024]{1,0:T(1,128)S(1)} %bitcast.6, f32[1,1024]{1,0:T(1,128)S(1)} %bitcast.7, s32[12,128]{1,0:T(8,128)S(1)} %bitcast.4, s32[12,128]{1,0:T(8,128)S(1)} %bitcast.5), custom_call_target="tpu_custom_call" | custom-call | flops 64487424 | tf_op jit(solution)/shard_map/pallas_call | solution.py:213
  32.3 0.6 %copy.10 = f32[6,1536]{1,0:T(8,128)} copy(f32[6,1536]{1,0:T(8,128)S(1)} %get-tuple-element.4) | data formatting | bytes 73728
  32.9 0.6 %copy.11 = f32[7,1536]{1,0:T(8,128)} copy(f32[7,1536]{1,0:T(8,128)S(1)} %get-tuple-element.5) | data formatting | bytes 86016
Async XLA Ops:
  0.6 0.7 %copy-start.4 = (f32[1024]{0:T(1024)S(1)}, f32[1024]{0:T(1024)}, u32[]{:S(2)}) copy-start(f32[1024]{0:T(1024)} %param.8) | copy-start | bytes 12292
  1.3 0.8 %copy-start = (f32[6,1024]{1,0:T(8,128)S(1)}, f32[6,1024]{1,0:T(8,128)}, u32[]{:S(2)}) copy-start(f32[6,1024]{1,0:T(8,128)} %pv.1) | copy-start | bytes 73732
  2.1 0.8 %copy-start.1 = (f32[6,1024]{1,0:T(8,128)S(1)}, f32[6,1024]{1,0:T(8,128)}, u32[]{:S(2)}) copy-start(f32[6,1024]{1,0:T(8,128)} %aj.1) | copy-start | bytes 73732
  2.8 0.7 %copy-start.2 = (s32[1536]{0:T(1024)S(1)}, s32[1536]{0:T(1024)}, u32[]{:S(2)}) copy-start(s32[1536]{0:T(1024)} %param.10) | copy-start | bytes 18436
  3.5 0.7 %copy-start.3 = (s32[1536]{0:T(1024)S(1)}, s32[1536]{0:T(1024)}, u32[]{:S(2)}) copy-start(s32[1536]{0:T(1024)} %param.11) | copy-start | bytes 18436
  4.2 0.7 %copy-start.5 = (f32[1024]{0:T(1024)S(1)}, f32[1024]{0:T(1024)}, u32[]{:S(2)}) copy-start(f32[1024]{0:T(1024)} %param.9) | copy-start | bytes 12292
